TPU v7x, 32 devices: a whole 2x2x4 slice. The times are simulated.
32 devices in a mesh: ifg: 16 (over z, y, x), tile: 2 (over core).
Axes of the slice: x: 2, y: 2, z: 4, core: 2. Of those that a mesh axis runs over, the one named last changes fastest.
Arguments:
- phases: float32 [1024, 128, 64], P('ifg', 'tile'), may hold values from -6 to 6
- pairs: int32 [1024, 2], replicated, may hold values from 0 to 299, as said below
- class_weights: float32 [8, 1024], replicated, may hold values from 0.05 to 1
- classes: int32 [128, 64], P('tile', 'ifg'), may hold values from 0 to 7
Outputs:
- corrected: float32 [128, 64, 300], P('tile', 'ifg')
Inputs may be any that keep to these rules, and one draw needn't show every extreme that they name: pairs[i,0] < pairs[i,1] <= pairs[i,0] + 8; some interferogram starts at date 0 and some ends at date 300 - 1.
All inputs are finite; a program needn't handle non-finite values.
Results may differ from a plain program's by a relative error of at most 0.0003.
Values sent between devices are 32-bit elements; how exact they have to be, the bound alone decides.
A program may use at most 128 MiB of HBM per device.

v0:
```python
import jax
import jax.numpy as jnp
from jax import lax
from jax.sharding import PartitionSpec as P

DATES = 300
CLASSES = 8
MAXGAP = 8
R = 3
smooth_weight = 1.0
anchor_weight = 0.1


def with_halo(cells, sides, width):
    for axis, dim in sides:
        count = lax.axis_size(axis)
        ends = count - 1
        head = lax.slice_in_dim(cells, 0, width, axis=dim)
        tail = lax.slice_in_dim(cells, cells.shape[dim] - width, cells.shape[dim], axis=dim)
        cells = jnp.concatenate(
            [
                lax.ppermute(tail, axis, [(i, (i + 1) % count) for i in range(ends)]),
                cells,
                lax.ppermute(head, axis, [((i + 1) % count, i) for i in range(ends)]),
            ],
            axis=dim,
        )
    return cells


def incidence_matrix(pairs):
    dates = jnp.arange(DATES, dtype=jnp.int32)[:, None]
    plus = (dates == pairs[:, 1][None, :]).astype(jnp.float32)
    minus = (dates == pairs[:, 0][None, :]).astype(jnp.float32)
    return (plus, minus)


def prior_matrix():
    second = jnp.arange(DATES - 2, dtype=jnp.int32)[:, None]
    columns = jnp.arange(DATES, dtype=jnp.int32)[None, :]
    diffs = (
        (columns == second).astype(jnp.float32)
        - 2.0 * (columns == second + 1).astype(jnp.float32)
        + (columns == second + 2).astype(jnp.float32)
    )
    curvature = jnp.dot(
        diffs.T, diffs, precision=lax.Precision.HIGHEST, preferred_element_type=jnp.float32
    )
    return smooth_weight * curvature + anchor_weight * jnp.eye(DATES, dtype=jnp.float32)


def class_systems(pairs, plus, minus, weights):
    diagonal = jnp.dot(
        weights,
        (plus + minus).T,
        precision=lax.Precision.HIGHEST,
        preferred_element_type=jnp.float32,
    )
    spacing = pairs[:, 1] - pairs[:, 0]
    offsets = jnp.arange(1, MAXGAP + 1, dtype=jnp.int32)[:, None]
    gap_onehot = (spacing[None, :] == offsets).astype(jnp.float32)
    spread = weights[:, None, :] * gap_onehot[None, :, :]
    band = jnp.einsum("kgi,ai->kga", spread, minus, precision=lax.Precision.HIGHEST)
    row_ids = jnp.arange(DATES, dtype=jnp.int32)[:, None]
    col_ids = jnp.arange(DATES, dtype=jnp.int32)[None, :]
    normal = diagonal[:, :, None] * (row_ids == col_ids).astype(jnp.float32)[None]
    for offset in range(MAXGAP):
        select = (col_ids == row_ids + offset + 1).astype(jnp.float32)
        normal = (
            normal
            - band[:, offset, :, None] * select[None]
            - band[:, offset, None, :] * select.T[None]
        )
    return normal


def invert(matrix):
    factor = jnp.linalg.cholesky(matrix)
    return jax.scipy.linalg.cho_solve((factor, True), jnp.eye(DATES, dtype=jnp.float32))


def filter_taps():
    offsets = jnp.arange(-R, R + 1).astype(jnp.float32)
    values = jnp.exp(-offsets * offsets / 4.5)
    return values / jnp.sum(values)


def pass_columns(padded, filter_weights, width):
    result = filter_weights[0] * padded[:, 0:width]
    for offset in range(1, 2 * R + 1):
        result = result + filter_weights[offset] * padded[:, offset : offset + width]
    return result


def pass_rows(padded, filter_weights, height):
    result = filter_weights[0] * padded[0:height]
    for offset in range(1, 2 * R + 1):
        result = result + filter_weights[offset] * padded[offset : offset + height]
    return result


def date_terms(received, incidence, weight_rows, onehot):
    flat = received.reshape(received.shape[0], -1)
    pixel_weights = jnp.dot(
        weight_rows, onehot, precision=lax.Precision.HIGHEST, preferred_element_type=jnp.float32
    )
    return jnp.einsum("ip,di->pd", pixel_weights * flat, incidence, precision=lax.Precision.HIGHEST)


def on_device(phases, pairs, class_weights, classes):
    plus, minus = incidence_matrix(pairs)
    incidence = plus - minus
    class_share = CLASSES // lax.axis_size("tile")
    first_class = lax.axis_index("tile") * class_share
    own_weights = lax.dynamic_slice_in_dim(class_weights, first_class, class_share, 0)
    own_normal = class_systems(pairs, plus, minus, own_weights)
    own_inverse = jax.vmap(invert)(own_normal + prior_matrix()[None])
    inverse = lax.all_gather(own_inverse, "tile", axis=0, tiled=True)
    tile_rows = phases.shape[1]
    tile_cols = classes.shape[1]
    class_flat = classes.reshape(-1)
    onehot = (class_flat[None, :] == jnp.arange(CLASSES, dtype=jnp.int32)[:, None]).astype(
        jnp.float32
    )
    weight_rows = class_weights.T
    regrouped = lax.all_to_all(phases, "ifg", split_axis=2, concat_axis=0, tiled=True)
    right_terms = date_terms(regrouped, incidence, weight_rows, onehot)
    solution = jnp.zeros((tile_rows * tile_cols, DATES), jnp.float32)
    for member in range(CLASSES):
        solved = jnp.einsum(
            "pd,ed->pe", right_terms, inverse[member], precision=lax.Precision.HIGHEST
        )
        solution = solution + onehot[member][:, None] * solved
    displacement = solution.reshape(tile_rows, tile_cols, DATES)
    filter_weights = filter_taps()
    padded = with_halo(displacement, (("ifg", 1), ("tile", 0)), R)
    across = pass_columns(padded, filter_weights, tile_cols)
    atmosphere = pass_rows(across, filter_weights, tile_rows)
    return displacement - atmosphere


def solution(mesh):
    return jax.shard_map(
        on_device,
        mesh=mesh,
        in_specs=(P("ifg", "tile", None), P(), P(), P("tile", "ifg")),
        out_specs=P("tile", "ifg", None),
        check_vma=False,
    )
```

profile of v0, /device:TPU:13, one launch (start us, length us, event | category | flops | bytes accessed | tf_op | source)
XLA Modules:
  0.0 464.6 jit_solution(6404731645494615155)
XLA Ops:
  7.3 1.3 fusion.6
  8.7 0.7 fusion.15
  9.5 1.4 bitcast_add_fusion
  12.6 4.8 %fusion.2 = f32[4,300,300]{2,1,0:T(8,128)S(1)} fusion(f32[300,300]{1,0:T(8,128)S(1)} %copy.75, f32[300,300]{1,0:T(8,128)S(1)} %copy.74, f32[4,300]{1,0:T(4,128)S(1)} %fusion.6, f32[300,300]{1,0:T(8,128)S(1)} %copy.73, f32[300,300]{1,0:T(8,128)S(1)} %get-tuple-element.96, f32[4,300]{1,0:T(4,128)S(1)} %get-tuple-element.82, ...), kind=kLoop, calls=%fused_computation.36 | loop fusion | flops 19440000 | bytes 8683200 | tf_op jit(solution)/shard_map/vmap(jit(cholesky))/div | solution.py:78
  17.4 1.3 copy-done.2
  18.7 46.9 %custom-call.29 = f32[4,128,128]{2,1,0:T(8,128)S(1)} custom-call(f32[4,128,128]{2,1,0:T(8,128)S(1)} %cholesky.205), custom_call_target="Cholesky" | custom-call | tf_op jit(solution)/shard_map/vmap(jit(cholesky))/cholesky | solution.py:78
  65.8 39.9 %custom-call.30 = f32[4,1,128,128]{2,3,1,0:T(8,128)} custom-call(f32[4,1,128,128]{3,2,1,0:T(8,128)S(1)} %select_bitcast_fusion.1), custom_call_target="InvertDiagBlocksLowerTriangular" | custom-call | tf_op jit(solution)/shard_map/vmap(jit(cholesky))/cholesky | solution.py:78
  105.7 1.5 constant_dynamic-update-slice_fusion.2
  107.2 1.7 convolution_subtract_fusion.3
  108.9 0.7 cholesky.209
  109.6 48.5 %custom-call.31 = f32[4,128,128]{2,1,0:T(8,128)} custom-call(f32[4,128,128]{2,1,0:T(8,128)} %cholesky.209), custom_call_target="Cholesky" | custom-call | tf_op jit(solution)/shard_map/vmap(jit(cholesky))/cholesky | solution.py:78
  158.1 1.7 select_reduce_fusion
  159.8 40.1 %custom-call.32 = f32[4,1,128,128]{2,3,1,0:T(8,128)S(1)} custom-call(f32[4,1,128,128]{3,2,1,0:T(8,128)} %get-tuple-element.31), custom_call_target="InvertDiagBlocksLowerTriangular" | custom-call | tf_op jit(solution)/shard_map/vmap(jit(cholesky))/cholesky | solution.py:78
  200.3 1.2 convolution_subtract_fusion.4
  201.5 16.1 %custom-call.33 = f32[4,44,44]{2,1,0:T(8,128)S(1)} custom-call(f32[4,44,44]{2,1,0:T(8,128)S(1)} %convolution_subtract_fusion.4), custom_call_target="Cholesky" | custom-call | tf_op jit(solution)/shard_map/vmap(jit(cholesky))/cholesky | solution.py:78
  218.0 0.9 copy-done.1
  218.9 1.8 select_select_fusion
  220.8 4.1 while.1
  220.8 0.6 fusion.131
  221.4 1.4 bitcast_dynamic-update-slice_fusion.2
  222.9 0.6 fusion.131
  223.5 1.4 bitcast_dynamic-update-slice_fusion.2
  225.1 118.7 %custom-call.34 = f32[4,3,128,128]{2,3,1,0:T(8,128)} custom-call(f32[4,3,128,128]{3,2,1,0:T(8,128)S(1)} %pad_maximum_fusion.2), custom_call_target="InvertDiagBlocksLowerTriangular" | custom-call | tf_op jit(solution)/shard_map/vmap(jit(_cho_solve))/triangular_solve | solution.py:79
  343.9 1.6 fusion.72
  345.6 0.7 convolution_subtract_fusion
  346.2 1.6 fusion.81
  348.0 1.3 fusion.24
  349.2 1.3 fusion.92
  350.6 1.3 fusion.91
  351.9 2.0 convolution_subtract_fusion.1
  354.2 1.8 fusion.80
  356.0 1.2 convolution_subtract_fusion.2
  357.2 1.6 fusion.79
  359.0 1.8 copy.89
  360.8 3.1 copy.69
  363.9 2.3 reshape.539
  366.2 6.9 %all-to-all-start = ((f32[16,1,16384]{2,1,0:T(1,128)}), f32[16,1,16384]{2,1,0:T(1,128)S(1)}, u32[]{:S(2)}, u32[]{:S(2)}) async-start(f32[16,1,16384]{2,1,0:T(1,128)} %reshape.539), calls=%async_computation | async-start | bytes 2097152 | tf_op jit(solution)/shard_map/all_to_all | solution.py:126
  373.4 24.5 %all-to-all-done = f32[16,1,16384]{2,1,0:T(1,128)S(1)} async-done(((f32[16,1,16384]{2,1,0:T(1,128)}), f32[16,1,16384]{2,1,0:T(1,128)S(1)}, u32[]{:S(2)}, u32[]{:S(2)}) %all-to-all-start) | async-done | bytes 1048608 | tf_op jit(solution)/shard_map/all_to_all | solution.py:126
  397.9 0.5 broadcast.592
  398.4 3.1 reduce.18
  401.6 0.8 reshape.540
  402.4 2.7 copy.70
  405.1 2.0 reshape.515
  407.1 0.6 fusion.4
  407.8 1.4 fusion.5
  409.2 1.8 convolution_multiply_fusion.6
  411.0 1.7 convolution_multiply_fusion.5
  412.7 1.7 convolution_multiply_fusion.4
  414.4 1.7 convolution_multiply_fusion.3
  416.1 0.7 convolution_multiply_fusion.2
  416.8 0.7 convolution_multiply_fusion.1
  417.5 0.7 convolution_multiply_fusion
  418.2 0.7 fusion.23
  419.3 2.1 collective-permute-start
  421.5 4.1 collective-permute-start.1
  425.5 0.6 fusion.99
  426.1 0.7 broadcast_divide_fusion
  426.8 4.2 collective-permute-done
  431.0 10.1 %collective-permute-done.1 = f32[64,3,300]{2,1,0:T(4,128)S(1)} collective-permute-done((f32[64,3,300]{2,1,0:T(4,128)S(1)}, f32[64,3,300]{2,1,0:T(4,128)S(1)}, u32[]{:S(2)}, u32[]{:S(2)}) %collective-permute-start.1) | collective-permute-done | bytes 230432 | tf_op jit(solution)/shard_map/ppermute | solution.py:24
  441.1 1.3 collective-permute-start.2
  442.4 3.0 collective-permute-start.3
  445.5 0.7 fusion.110
  446.8 5.0 %fusion.56 = f32[70,4,300]{2,1,0:T(4,128)S(1)} fusion(f32[70,10,300]{2,1,0:T(8,128)S(1)} %pad_maximum_fusion.1, f32[]{:T(128)} %bitcast.39, f32[]{:T(128)} %bitcast.38, f32[]{:T(128)} %bitcast.37, f32[]{:T(128)} %bitcast.36, f32[]{:T(128)} %bitcast.35, f32[]{:T(128)} %bitcast.34, f32[]{:T(128)} %bitcast.33), kind=kLoop, calls=%fused_computation.143 | loop fusion | flops 1092000 | bytes 2688028 | tf_op jit(solution)/shard_map/add | solution.py:91
  451.8 5.5 %fusion.63 = f32[64,4,300]{2,1,0:T(4,128)} fusion(f32[64,4,300]{2,1,0:T(4,128)S(1)} %reshape.516, f32[70,4,300]{2,1,0:T(4,128)S(1)} %fusion.56, f32[]{:T(128)} %bitcast.39, f32[]{:T(128)} %bitcast.38, f32[]{:T(128)} %bitcast.37, f32[]{:T(128)} %bitcast.36, f32[]{:T(128)} %bitcast.35, f32[]{:T(128)} %bitcast.34, f32[]{:T(128)} %bitcast.33), kind=kLoop, calls=%fused_computation.157 | loop fusion | flops 1075200 | bytes 2764828 | tf_op jit(solution)/shard_map/sub | solution.py:139
  (86 shorter events, 5.5 us)
Async XLA Ops:
  6.5 0.8 copy-start
  6.5 0.7 copy-start.5
  6.5 402.6 %all-gather.2.cloned.1.call-start = ((), (), s32[]{:S(2)}) async-start(), calls=%async_computation.1 | async-start | bytes 5603328 | tf_op jit(solution)/shard_map/all_gather | solution.py:118
  6.7 2.7 copy-start.3
  17.4 1.3 copy-start.2
  217.7 1.3 copy-start.1
  343.9 4.0 slice-start
  363.9 9.3 %copy-start.6 = (s32[64,4]{0,1:T(4,128)S(1)}, s32[64,4]{0,1:T(4,128)}, u32[]{:S(2)}) copy-start(s32[64,4]{0,1:T(4,128)} %param.7) | copy-start | bytes 3076
  366.2 31.7 %all-to-all-start = ((f32[16,1,16384]{2,1,0:T(1,128)}), f32[16,1,16384]{2,1,0:T(1,128)S(1)}, u32[]{:S(2)}, u32[]{:S(2)}) async-start(f32[16,1,16384]{2,1,0:T(1,128)} %reshape.539), calls=%async_computation | async-start | bytes 2097152 | tf_op jit(solution)/shard_map/all_to_all | solution.py:126
  409.2 6.9 %copy-start.4 = (f32[8,300,300]{2,1,0:T(8,128)S(1)}, f32[8,300,300]{2,1,0:T(8,128)}, u32[]{:S(2)}) copy-start(f32[8,300,300]{2,1,0:T(8,128)} %all-gather.2.cloned.1.call-done) | copy-start | bytes 8640004
  419.3 11.7 %collective-permute-start = (f32[64,3,300]{2,1,0:T(4,128)S(1)}, f32[64,3,300]{2,1,0:T(4,128)S(1)}, u32[]{:S(2)}, u32[]{:S(2)}) collective-permute-start(f32[64,3,300]{2,1,0:T(4,128)S(1)} %get-tuple-element.29), channel_id=1, source_target_pairs={{0,2},{2,4},{4,6},{6,8},{8,10},{10,12},{12,14},{14,16},{16,18},{18... | collective-permute-start | bytes 691208 | tf_op jit(solution)/shard_map/ppermute | solution.py:22
  421.5 19.6 %collective-permute-start.1 = (f32[64,3,300]{2,1,0:T(4,128)S(1)}, f32[64,3,300]{2,1,0:T(4,128)S(1)}, u32[]{:S(2)}, u32[]{:S(2)}) collective-permute-start(f32[64,3,300]{2,1,0:T(4,128)S(1)} %get-tuple-element.30), channel_id=1, source_target_pairs={{2,0},{4,2},{6,4},{8,6},{10,8},{12,10},{14,12},{16,14},{18,16},{20... | collective-permute-start | bytes 691208 | tf_op jit(solution)/shard_map/ppermute | solution.py:24
  441.1 5.0 %collective-permute-start.2 = (f32[3,10,300]{2,1,0:T(8,128)S(1)}, f32[3,10,300]{2,1,0:T(8,128)S(1)}, u32[]{:S(2)}, u32[]{:S(2)}) collective-permute-start(f32[3,10,300]{2,1,0:T(8,128)S(1)} %get-tuple-element.25), channel_id=1, source_target_pairs={{0,1},{2,3},{4,5},{6,7},{8,9},{10,11},{12,13},{14,15},{16,17},{18,... | collective-permute-start | bytes 108008 | tf_op jit(solution)/shard_map/ppermute | solution.py:22
  442.4 3.9 collective-permute-start.3
Sparse Core Ops, SparseCore 0:
  360.9 14.8 all-gather.1
where the time goes:
time: 470 us; the launch traced here: 465 us
  other arithmetic  336 us (71%)
  waiting for transfers between devices  39 us (8%)
  matrix products  34.2 us (7%)
  local copies, waits for them, and re-layouts  23.4 us (5%)
  starting transfers between devices  17.5 us (4%)
  between operations  14.6 us (3%)
    another operation x14, other arithmetic, invert(): factor = jnp.linalg.cholesky(matrix)  194 us
    another operation x9, other arithmetic, invert(): jax.scipy.linalg.cho_solve((factor, True), jnp.eye(DATES, dtype=jnp.float...  121 us
    all_to_all x1, waiting for transfers between devices, on_device(): lax.all_to_all(phases, 'ifg', split_axis=2, concat_axis=0, tiled=True)  24.5 us
    another operation x10, matrix products, invert(): jax.scipy.linalg.cho_solve((factor, True), jnp.eye(DATES, dtype=jnp.float...  14.5 us
    ppermute x2, waiting for transfers between devices, with_halo(): lax.ppermute(head, axis, [((i + 1) % count, i) for i in range(ends)])  10.3 us
    dot_general x8, matrix products, on_device(): jnp.einsum('pd,ed->pe', right_terms, inverse[member], precision=lax.Preci...  9.61 us
  transfers between devices with their start and end apart: 6, of which 4 were waited for; matrix products, arithmetic and copies ran while one was open for 4% of the time, Pallas kernels for 0%

commit v1 on v0

--- a/solution.py
+++ b/solution.py
@@ -9,6 +9,25 @@
 R = 3
 smooth_weight = 1.0
 anchor_weight = 0.1
+
+
+def convert_steps_all(panel, d_out, join_dim):
+    reached = lax.axis_size("ifg")
+    step_out, earlier = (reached, lax.axis_index("ifg"))
+    current_block = panel.shape[d_out] // step_out
+    carry_out = jnp.roll(panel, -earlier * current_block, d_out)
+    trail = [lax.slice_in_dim(carry_out, 0, current_block, axis=d_out)]
+    idx = 1
+    while idx < step_out:
+        item_now = lax.slice_in_dim(
+            carry_out, idx * current_block, (idx + 1) * current_block, axis=d_out
+        )
+        y_new = lax.ppermute(item_now, "ifg", [(c, (c + idx) % step_out) for c in range(step_out)])
+        trail.append(y_new)
+        idx += 1
+    return jnp.roll(
+        jnp.concatenate(trail[::-1], join_dim), (earlier + 1) * trail[0].shape[join_dim], join_dim
+    )
 
 
 def with_halo(cells, sides, width):
@@ -123,7 +142,7 @@
         jnp.float32
     )
     weight_rows = class_weights.T
-    regrouped = lax.all_to_all(phases, "ifg", split_axis=2, concat_axis=0, tiled=True)
+    regrouped = convert_steps_all(phases, 2, 0)
     right_terms = date_terms(regrouped, incidence, weight_rows, onehot)
     solution = jnp.zeros((tile_rows * tile_cols, DATES), jnp.float32)
     for member in range(CLASSES):

time: 470 us -> 502 us (1.068)
  starting transfers between devices: 17.5 us -> 51.7 us
  waiting for transfers between devices: 39 us -> 22.4 us
  local copies, waits for them, and re-layouts: 23.4 us -> 37.8 us
    ppermute x0 -> x15, starting transfers between devices: none -> 39.6 us  [convert_steps_all(): lax.ppermute(item_now, 'ifg', [(c, (c + idx) % step_out) for c in range(s...]
    all_to_all x1 -> x0, waiting for transfers between devices: 24.5 us -> none  [on_device(): lax.all_to_all(phases, 'ifg', split_axis=2, concat_axis=0, tiled=True)]
    ppermute x0 -> x15, local copies, waits for them, and re-layouts: none -> 15.2 us  [convert_steps_all(): lax.ppermute(item_now, 'ifg', [(c, (c + idx) % step_out) for c in range(s...]
    ppermute x0 -> x15, waiting for transfers between devices: none -> 8.11 us  [convert_steps_all(): lax.ppermute(item_now, 'ifg', [(c, (c + idx) % step_out) for c in range(s...]
    all_to_all x1 -> x0, starting transfers between devices: 6.95 us -> none  [on_device(): lax.all_to_all(phases, 'ifg', split_axis=2, concat_axis=0, tiled=True)]
  transfers between devices with their start and end apart: 6 -> 20, of which waited for: 4 -> 6; matrix products, arithmetic and copies ran while one was open for 4% -> 6% of each run, Pallas kernels for 0% -> 0%
where the time goes in v1:
time: 502 us; the launch traced here: 494 us
  other arithmetic  334 us (67%)
  starting transfers between devices  51.7 us (10%)
  local copies, waits for them, and re-layouts  37.8 us (8%)
  matrix products  34.3 us (7%)
  waiting for transfers between devices  22.4 us (4%)
  between operations  14.4 us (3%)
    another operation x14, other arithmetic, invert(): factor = jnp.linalg.cholesky(matrix)  194 us
    another operation x9, other arithmetic, invert(): jax.scipy.linalg.cho_solve((factor, True), jnp.eye(DATES, dtype=jnp.float...  121 us
    ppermute x15, starting transfers between devices, convert_steps_all(): lax.ppermute(item_now, 'ifg', [(c, (c + idx) % step_out) for c in range(s...  39.6 us
    ppermute x15, local copies, waits for them, and re-layouts, convert_steps_all(): lax.ppermute(item_now, 'ifg', [(c, (c + idx) % step_out) for c in range(s...  15.2 us
    another operation x10, matrix products, invert(): jax.scipy.linalg.cho_solve((factor, True), jnp.eye(DATES, dtype=jnp.float...  14.5 us
    ppermute x2, waiting for transfers between devices, with_halo(): lax.ppermute(head, axis, [((i + 1) % count, i) for i in range(ends)])  12.7 us
  transfers between devices with their start and end apart: 20, of which 6 were waited for; matrix products, arithmetic and copies ran while one was open for 6% of the time, Pallas kernels for 0%

profile of v1, /device:TPU:13, one launch (start us, length us, event | category | flops | bytes accessed | tf_op | source)
XLA Modules:
  0.0 494.2 jit_solution(11012547785174135596)
XLA Ops:
  7.3 1.3 fusion.6
  9.5 1.4 bitcast_add_fusion
  12.6 4.5 fusion.3
  17.1 1.2 copy-done.2
  18.4 46.9 %custom-call.29 = f32[4,128,128]{2,1,0:T(8,128)S(1)} custom-call(f32[4,128,128]{2,1,0:T(8,128)S(1)} %cholesky.205), custom_call_target="Cholesky" | custom-call | tf_op jit(solution)/shard_map/vmap(jit(cholesky))/cholesky | solution.py:97
  65.5 39.9 %custom-call.30 = f32[4,1,128,128]{2,3,1,0:T(8,128)} custom-call(f32[4,1,128,128]{3,2,1,0:T(8,128)S(1)} %select_bitcast_fusion.1), custom_call_target="InvertDiagBlocksLowerTriangular" | custom-call | tf_op jit(solution)/shard_map/vmap(jit(cholesky))/cholesky | solution.py:97
  105.4 1.5 constant_dynamic-update-slice_fusion.2
  106.9 1.7 convolution_subtract_fusion.3
  109.3 48.5 %custom-call.31 = f32[4,128,128]{2,1,0:T(8,128)} custom-call(f32[4,128,128]{2,1,0:T(8,128)} %cholesky.209), custom_call_target="Cholesky" | custom-call | tf_op jit(solution)/shard_map/vmap(jit(cholesky))/cholesky | solution.py:97
  157.9 1.7 select_reduce_fusion
  159.6 40.1 %custom-call.32 = f32[4,1,128,128]{2,3,1,0:T(8,128)S(1)} custom-call(f32[4,1,128,128]{3,2,1,0:T(8,128)} %get-tuple-element.47), custom_call_target="InvertDiagBlocksLowerTriangular" | custom-call | tf_op jit(solution)/shard_map/vmap(jit(cholesky))/cholesky | solution.py:97
  200.0 1.2 convolution_subtract_fusion.4
  201.2 16.1 %custom-call.33 = f32[4,44,44]{2,1,0:T(8,128)S(1)} custom-call(f32[4,44,44]{2,1,0:T(8,128)S(1)} %convolution_subtract_fusion.4), custom_call_target="Cholesky" | custom-call | tf_op jit(solution)/shard_map/vmap(jit(cholesky))/cholesky | solution.py:97
  218.7 1.8 select_select_fusion
  220.5 3.9 while.1
  221.1 1.4 bitcast_dynamic-update-slice_fusion.2
  223.1 1.4 bitcast_dynamic-update-slice_fusion.2
  224.7 118.9 %custom-call.34 = f32[4,3,128,128]{2,3,1,0:T(8,128)} custom-call(f32[4,3,128,128]{3,2,1,0:T(8,128)S(1)} %pad_maximum_fusion.2), custom_call_target="InvertDiagBlocksLowerTriangular" | custom-call | tf_op jit(solution)/shard_map/vmap(jit(_cho_solve))/triangular_solve | solution.py:98
  343.7 1.6 fusion.73
  346.0 1.6 fusion.82
  347.8 1.3 fusion.24
  349.1 1.3 fusion.93
  350.4 1.3 fusion.92
  351.7 2.0 convolution_subtract_fusion.1
  354.0 1.8 fusion.81
  355.8 1.2 convolution_subtract_fusion.2
  357.0 1.6 fusion.80
  358.8 1.8 copy.154
  360.7 3.1 copy.101
  363.8 0.9 fusion
  364.9 1.2 collective-permute-start
  366.1 1.1 collective-permute-start.1
  367.2 3.3 collective-permute-start.3
  370.5 2.1 collective-permute-start.4
  374.1 3.4 collective-permute-start.6
  377.5 2.0 collective-permute-start.7
  379.5 3.0 collective-permute-start.8
  382.5 2.1 collective-permute-start.9
  384.6 1.7 collective-permute-done.5
  386.3 0.9 collective-permute-start.10
  387.2 5.9 %collective-permute-done.6 = f32[64,64,4]{1,0,2:T(8,128)S(1)} collective-permute-done((f32[64,64,4]{1,0,2:T(8,128)S(1)}, f32[64,64,4]{1,0,2:T(8,128)S(1)}, u32[]{:S(2)}, u32[]{:S(2)}) %collective-permute-start.6) | collective-permute-done | bytes 65568 | tf_op jit(solution)/shard_map/ppermute | solution.py:25
  393.1 8.2 %collective-permute-start.11 = (f32[64,64,4]{1,0,2:T(8,128)S(1)}, f32[64,64,4]{1,0,2:T(8,128)S(1)}, u32[]{:S(2)}, u32[]{:S(2)}) collective-permute-start(f32[64,64,4]{1,0,2:T(8,128)S(1)} %get-tuple-element.29), channel_id=1, source_target_pairs={{0,8},{2,10},{4,12},{6,14},{8,16},{10,18},{12,20},{14,22},{16,24},... | collective-permute-start | bytes 196616 | tf_op jit(solution)/shard_map/ppermute | solution.py:25
  401.4 11.6 %collective-permute-start.12 = (f32[64,64,4]{1,0,2:T(8,128)S(1)}, f32[64,64,4]{1,0,2:T(8,128)S(1)}, u32[]{:S(2)}, u32[]{:S(2)}) collective-permute-start(f32[64,64,4]{1,0,2:T(8,128)S(1)} %get-tuple-element.28), channel_id=1, source_target_pairs={{0,6},{2,8},{4,10},{6,12},{8,14},{10,16},{12,18},{14,20},{16,22},{... | collective-permute-start | bytes 196616 | tf_op jit(solution)/shard_map/ppermute | solution.py:25
  413.6 1.0 copy.103
  414.7 1.7 copy.104
  416.3 1.7 copy.105
  418.0 1.7 copy.106
  419.6 1.7 copy.107
  428.8 3.8 concatenate.43
  433.0 1.7 copy.135
  434.7 1.6 reshape.514
  436.3 1.4 fusion.5
  437.7 1.8 convolution_multiply_fusion.6
  439.6 1.7 convolution_multiply_fusion.5
  441.3 1.7 convolution_multiply_fusion.4
  443.0 1.7 convolution_multiply_fusion.3
  447.9 5.8 %collective-permute-start.15 = (f32[64,3,300]{2,1,0:T(4,128)S(1)}, f32[64,3,300]{2,1,0:T(4,128)S(1)}, u32[]{:S(2)}, u32[]{:S(2)}) collective-permute-start(f32[64,3,300]{2,1,0:T(4,128)S(1)} %get-tuple-element.45), channel_id=1, source_target_pairs={{0,2},{2,4},{4,6},{6,8},{8,10},{10,12},{12,14},{14,16},{16,18},{18... | collective-permute-start | bytes 691208 | tf_op jit(solution)/shard_map/ppermute | solution.py:41
  453.7 1.9 collective-permute-start.16
  456.9 1.5 collective-permute-done.15
  458.4 12.5 %collective-permute-done.16 = f32[64,3,300]{2,1,0:T(4,128)S(1)} collective-permute-done((f32[64,3,300]{2,1,0:T(4,128)S(1)}, f32[64,3,300]{2,1,0:T(4,128)S(1)}, u32[]{:S(2)}, u32[]{:S(2)}) %collective-permute-start.16) | collective-permute-done | bytes 230432 | tf_op jit(solution)/shard_map/ppermute | solution.py:43
  471.0 1.3 collective-permute-start.17
  472.3 3.0 collective-permute-start.18
  476.6 5.1 %fusion.57 = f32[70,4,300]{2,1,0:T(4,128)S(1)} fusion(f32[70,10,300]{2,1,0:T(8,128)S(1)} %pad_maximum_fusion.1, f32[]{:T(128)} %bitcast.37, f32[]{:T(128)} %bitcast.36, f32[]{:T(128)} %bitcast.35, f32[]{:T(128)} %bitcast.34, f32[]{:T(128)} %bitcast.33, f32[]{:T(128)} %bitcast.32, f32[]{:T(128)} %bitcast.31), kind=kLoop, calls=%fused_computation.146 | loop fusion | flops 1092000 | bytes 2688028 | tf_op jit(solution)/shard_map/add | solution.py:110
  481.7 5.5 %fusion.64 = f32[64,4,300]{2,1,0:T(4,128)} fusion(f32[64,4,300]{2,1,0:T(4,128)S(1)} %reshape.515, f32[70,4,300]{2,1,0:T(4,128)S(1)} %fusion.57, f32[]{:T(128)} %bitcast.37, f32[]{:T(128)} %bitcast.36, f32[]{:T(128)} %bitcast.35, f32[]{:T(128)} %bitcast.34, f32[]{:T(128)} %bitcast.33, f32[]{:T(128)} %bitcast.32, f32[]{:T(128)} %bitcast.31), kind=kLoop, calls=%fused_computation.160 | loop fusion | flops 1075200 | bytes 2764828 | tf_op jit(solution)/shard_map/sub | solution.py:158
  (134 shorter events, 24.1 us)
Async XLA Ops:
  6.5 0.8 copy-start
  6.5 0.7 copy-start.7
  6.5 431.2 %all-gather.2.cloned.1.call-start = ((), (), s32[]{:S(2)}) async-start(), calls=%async_computation | async-start | bytes 5603328 | tf_op jit(solution)/shard_map/all_gather | solution.py:137
  6.7 2.7 copy-start.3
  17.1 1.3 copy-start.2
  217.4 1.3 copy-start.1
  343.7 4.0 slice-start
  364.7 8.0 %copy-start.8 = (s32[64,4]{0,1:T(4,128)S(1)}, s32[64,4]{0,1:T(4,128)}, u32[]{:S(2)}) copy-start(s32[64,4]{0,1:T(4,128)} %param.7) | copy-start | bytes 3076
  364.9 8.6 %collective-permute-start = (f32[64,64,4]{1,0,2:T(8,128)S(1)}, f32[64,64,4]{1,0,2:T(8,128)S(1)}, u32[]{:S(2)}, u32[]{:S(2)}) collective-permute-start(f32[64,64,4]{1,0,2:T(8,128)S(1)} %get-tuple-element.40), channel_id=1, source_target_pairs={{0,30},{2,0},{4,2},{6,4},{8,6},{10,8},{12,10},{14,12},{16,14},{18,... | collective-permute-start | bytes 196616 | tf_op jit(solution)/shard_map/ppermute | solution.py:25
  366.1 8.0 %collective-permute-start.1 = (f32[64,64,4]{1,0,2:T(8,128)S(1)}, f32[64,64,4]{1,0,2:T(8,128)S(1)}, u32[]{:S(2)}, u32[]{:S(2)}) collective-permute-start(f32[64,64,4]{1,0,2:T(8,128)S(1)} %get-tuple-element.39), channel_id=1, source_target_pairs={{0,28},{2,30},{4,0},{6,2},{8,4},{10,6},{12,8},{14,10},{16,12},{18,... | collective-permute-start | bytes 196616 | tf_op jit(solution)/shard_map/ppermute | solution.py:25
  367.2 10.3 %collective-permute-start.2 = (f32[64,64,4]{1,0,2:T(8,128)S(1)}, f32[64,64,4]{1,0,2:T(8,128)}, u32[]{:S(2)}, u32[]{:S(2)}) collective-permute-start(f32[64,64,4]{1,0,2:T(8,128)S(1)} %get-tuple-element.38), channel_id=1, source_target_pairs={{0,26},{2,28},{4,30},{6,0},{8,2},{10,4},{12,6},{14,8},{16,10},{18,... | collective-permute-start | bytes 196616 | tf_op jit(solution)/shard_map/ppermute | solution.py:25
  367.2 12.3 %collective-permute-start.3 = (f32[64,64,4]{1,0,2:T(8,128)S(1)}, f32[64,64,4]{1,0,2:T(8,128)}, u32[]{:S(2)}, u32[]{:S(2)}) collective-permute-start(f32[64,64,4]{1,0,2:T(8,128)S(1)} %get-tuple-element.37), channel_id=1, source_target_pairs={{0,24},{2,26},{4,28},{6,30},{8,0},{10,2},{12,4},{14,6},{16,8},{18,... | collective-permute-start | bytes 196616 | tf_op jit(solution)/shard_map/ppermute | solution.py:25
  370.5 11.9 %collective-permute-start.4 = (f32[64,64,4]{1,0,2:T(8,128)S(1)}, f32[64,64,4]{1,0,2:T(8,128)}, u32[]{:S(2)}, u32[]{:S(2)}) collective-permute-start(f32[64,64,4]{1,0,2:T(8,128)S(1)} %get-tuple-element.36), channel_id=1, source_target_pairs={{0,22},{2,24},{4,26},{6,28},{8,30},{10,0},{12,2},{14,4},{16,6},{18... | collective-permute-start | bytes 196616 | tf_op jit(solution)/shard_map/ppermute | solution.py:25
  373.5 40.0 %copy-start.5 = (f32[64,64,4]{1,0,2:T(8,128)}, f32[64,64,4]{1,0,2:T(8,128)S(1)}, u32[]{:S(2)}) copy-start(f32[64,64,4]{1,0,2:T(8,128)S(1)} %collective-permute-done) | copy-start | bytes 196612
  373.5 12.8 %collective-permute-start.5 = (f32[64,64,4]{1,0,2:T(8,128)S(1)}, f32[64,64,4]{1,0,2:T(8,128)S(1)}, u32[]{:S(2)}, u32[]{:S(2)}) collective-permute-start(f32[64,64,4]{1,0,2:T(8,128)S(1)} %get-tuple-element.35), channel_id=1, source_target_pairs={{0,20},{2,22},{4,24},{6,26},{8,28},{10,30},{12,0},{14,2},{16,4},{1... | collective-permute-start | bytes 196616 | tf_op jit(solution)/shard_map/ppermute | solution.py:25
  374.1 39.6 %copy-start.6 = (f32[64,64,4]{1,0,2:T(8,128)}, f32[64,64,4]{1,0,2:T(8,128)S(1)}, u32[]{:S(2)}) copy-start(f32[64,64,4]{1,0,2:T(8,128)S(1)} %collective-permute-done.1) | copy-start | bytes 196612
  374.1 19.1 %collective-permute-start.6 = (f32[64,64,4]{1,0,2:T(8,128)S(1)}, f32[64,64,4]{1,0,2:T(8,128)S(1)}, u32[]{:S(2)}, u32[]{:S(2)}) collective-permute-start(f32[64,64,4]{1,0,2:T(8,128)S(1)} %get-tuple-element.34), channel_id=1, source_target_pairs={{0,18},{2,20},{4,22},{6,24},{8,26},{10,28},{12,30},{14,0},{16,2},{... | collective-permute-start | bytes 196616 | tf_op jit(solution)/shard_map/ppermute | solution.py:25
  377.5 23.9 %collective-permute-start.7 = (f32[64,64,4]{1,0,2:T(8,128)S(1)}, f32[64,64,4]{1,0,2:T(8,128)S(1)}, u32[]{:S(2)}, u32[]{:S(2)}) collective-permute-start(f32[64,64,4]{1,0,2:T(8,128)S(1)} %get-tuple-element.33), channel_id=1, source_target_pairs={{0,16},{2,18},{4,20},{6,22},{8,24},{10,26},{12,28},{14,30},{16,0},... | collective-permute-start | bytes 196616 | tf_op jit(solution)/shard_map/ppermute | solution.py:25
  379.5 33.5 %collective-permute-start.8 = (f32[64,64,4]{1,0,2:T(8,128)S(1)}, f32[64,64,4]{1,0,2:T(8,128)S(1)}, u32[]{:S(2)}, u32[]{:S(2)}) collective-permute-start(f32[64,64,4]{1,0,2:T(8,128)S(1)} %get-tuple-element.32), channel_id=1, source_target_pairs={{0,14},{2,16},{4,18},{6,20},{8,22},{10,24},{12,26},{14,28},{16,30}... | collective-permute-start | bytes 196616 | tf_op jit(solution)/shard_map/ppermute | solution.py:25
  382.5 30.5 %collective-permute-start.9 = (f32[64,64,4]{1,0,2:T(8,128)S(1)}, f32[64,64,4]{1,0,2:T(8,128)S(1)}, u32[]{:S(2)}, u32[]{:S(2)}) collective-permute-start(f32[64,64,4]{1,0,2:T(8,128)S(1)} %get-tuple-element.31), channel_id=1, source_target_pairs={{0,12},{2,14},{4,16},{6,18},{8,20},{10,22},{12,24},{14,26},{16,28}... | collective-permute-start | bytes 196616 | tf_op jit(solution)/shard_map/ppermute | solution.py:25
  386.3 38.7 %collective-permute-start.10 = (f32[64,64,4]{1,0,2:T(8,128)S(1)}, f32[64,64,4]{1,0,2:T(8,128)S(1)}, u32[]{:S(2)}, u32[]{:S(2)}) collective-permute-start(f32[64,64,4]{1,0,2:T(8,128)S(1)} %get-tuple-element.30), channel_id=1, source_target_pairs={{0,10},{2,12},{4,14},{6,16},{8,18},{10,20},{12,22},{14,24},{16,26}... | collective-permute-start | bytes 196616 | tf_op jit(solution)/shard_map/ppermute | solution.py:25
  393.1 32.7 %collective-permute-start.11 = (f32[64,64,4]{1,0,2:T(8,128)S(1)}, f32[64,64,4]{1,0,2:T(8,128)S(1)}, u32[]{:S(2)}, u32[]{:S(2)}) collective-permute-start(f32[64,64,4]{1,0,2:T(8,128)S(1)} %get-tuple-element.29), channel_id=1, source_target_pairs={{0,8},{2,10},{4,12},{6,14},{8,16},{10,18},{12,20},{14,22},{16,24},... | collective-permute-start | bytes 196616 | tf_op jit(solution)/shard_map/ppermute | solution.py:25
  401.4 25.2 %collective-permute-start.12 = (f32[64,64,4]{1,0,2:T(8,128)S(1)}, f32[64,64,4]{1,0,2:T(8,128)S(1)}, u32[]{:S(2)}, u32[]{:S(2)}) collective-permute-start(f32[64,64,4]{1,0,2:T(8,128)S(1)} %get-tuple-element.28), channel_id=1, source_target_pairs={{0,6},{2,8},{4,10},{6,12},{8,14},{10,16},{12,18},{14,20},{16,22},{... | collective-permute-start | bytes 196616 | tf_op jit(solution)/shard_map/ppermute | solution.py:25
  413.0 14.3 %collective-permute-start.13 = (f32[64,64,4]{1,0,2:T(8,128)S(1)}, f32[64,64,4]{1,0,2:T(8,128)S(1)}, u32[]{:S(2)}, u32[]{:S(2)}) collective-permute-start(f32[64,64,4]{1,0,2:T(8,128)S(1)} %get-tuple-element.27), channel_id=1, source_target_pairs={{0,4},{2,6},{4,8},{6,10},{8,12},{10,14},{12,16},{14,18},{16,20},{1... | collective-permute-start | bytes 196616 | tf_op jit(solution)/shard_map/ppermute | solution.py:25
  413.0 15.1 %collective-permute-start.14 = (f32[64,64,4]{1,0,2:T(8,128)S(1)}, f32[64,64,4]{1,0,2:T(8,128)S(1)}, u32[]{:S(2)}, u32[]{:S(2)}) collective-permute-start(f32[64,64,4]{1,0,2:T(8,128)S(1)} %get-tuple-element.26), channel_id=1, source_target_pairs={{0,2},{2,4},{4,6},{6,8},{8,10},{10,12},{12,14},{14,16},{16,18},{18... | collective-permute-start | bytes 196616 | tf_op jit(solution)/shard_map/ppermute | solution.py:25
  437.7 7.0 %copy-start.4 = (f32[8,300,300]{2,1,0:T(8,128)S(1)}, f32[8,300,300]{2,1,0:T(8,128)}, u32[]{:S(2)}) copy-start(f32[8,300,300]{2,1,0:T(8,128)} %all-gather.2.cloned.1.call-done) | copy-start | bytes 8640004
  447.9 10.5 %collective-permute-start.15 = (f32[64,3,300]{2,1,0:T(4,128)S(1)}, f32[64,3,300]{2,1,0:T(4,128)S(1)}, u32[]{:S(2)}, u32[]{:S(2)}) collective-permute-start(f32[64,3,300]{2,1,0:T(4,128)S(1)} %get-tuple-element.45), channel_id=1, source_target_pairs={{0,2},{2,4},{4,6},{6,8},{8,10},{10,12},{12,14},{14,16},{16,18},{18... | collective-permute-start | bytes 691208 | tf_op jit(solution)/shard_map/ppermute | solution.py:41
  453.7 17.2 %collective-permute-start.16 = (f32[64,3,300]{2,1,0:T(4,128)S(1)}, f32[64,3,300]{2,1,0:T(4,128)S(1)}, u32[]{:S(2)}, u32[]{:S(2)}) collective-permute-start(f32[64,3,300]{2,1,0:T(4,128)S(1)} %get-tuple-element.46), channel_id=1, source_target_pairs={{2,0},{4,2},{6,4},{8,6},{10,8},{12,10},{14,12},{16,14},{18,16},{20... | collective-permute-start | bytes 691208 | tf_op jit(solution)/shard_map/ppermute | solution.py:43
  471.0 5.0 %collective-permute-start.17 = (f32[3,10,300]{2,1,0:T(8,128)S(1)}, f32[3,10,300]{2,1,0:T(8,128)S(1)}, u32[]{:S(2)}, u32[]{:S(2)}) collective-permute-start(f32[3,10,300]{2,1,0:T(8,128)S(1)} %get-tuple-element.41), channel_id=1, source_target_pairs={{0,1},{2,3},{4,5},{6,7},{8,9},{10,11},{12,13},{14,15},{16,17},{18,... | collective-permute-start | bytes 108008 | tf_op jit(solution)/shard_map/ppermute | solution.py:41
  472.3 3.9 collective-permute-start.18
Sparse Core Ops, SparseCore 0:
  360.8 14.8 all-gather.1
